TPU v7x, 128 devices: a whole 4x4x4 slice. The times are simulated.
128 devices in a mesh: fsdp: 16 (over y, z), tp: 8 (over x, core).
Axes of the slice: x: 4, y: 4, z: 4, core: 2. Of those that a mesh axis runs over, the one named last changes fastest.
Arguments:
- tokens: bfloat16 [4096, 4096], P('fsdp', 'tp'), may hold values from -6 to 6
- gate_tiles: bfloat16 [288, 1024, 128], P('fsdp', 'tp'), may hold values from -0.125 to 0.125
- up_tiles: bfloat16 [288, 1024, 128], P('fsdp', 'tp'), may hold values from -0.125 to 0.125
- gate_slots: int32 [288, 8], P(None, 'tp'), may hold values from -1 to 27, as said below
- up_slots: int32 [288, 8], P(None, 'tp'), may hold values from -1 to 27, as said below
- cotangent: bfloat16 [4096, 14336], P('fsdp', 'tp'), may hold values from -6 to 6
Outputs:
- hidden: bfloat16 [4096, 14336], P('fsdp', 'tp')
- input_grad: bfloat16 [4096, 4096], P('fsdp', 'tp')
- gate_tile_grad: bfloat16 [288, 1024, 128], P('fsdp', 'tp')
- up_tile_grad: bfloat16 [288, 1024, 128], P('fsdp', 'tp')
Inputs may be any that keep to these rules, and one draw needn't show every extreme that they name: `gate_slots`: for each owner (rows f * 18 to (f + 1) * 18 - 1, column t) the non-negative entries are distinct positions of that owner, stand before its -1 entries, and number 10 to 18; in every draw some owner fills all 18 slots. `up_slots`: as for gate_slots, drawn independently.
All inputs are finite; a program needn't handle non-finite values.
Results may differ from a plain program's by a relative error of at most 0.02.
Values may be sent and summed in bfloat16 or wider, within the bound.
No kernel may reach another device: no remote copies, remote signals or barrier semaphores. Data moves between devices by JAX's collectives and lax.ppermute only.
A program may use at most 192 MiB of HBM per device.

v0:
```python
import jax
import jax.numpy as jnp
from jax import lax
from jax.sharding import PartitionSpec as P


def per_device(tokens, gate_tiles, up_tiles, gate_slots, up_slots, cotangent):
    n_fsdp = lax.axis_size("fsdp")
    n_tp = lax.axis_size("tp")
    tile_size = gate_tiles.shape[-1]
    capacity = gate_tiles.shape[0]
    tok_rows = tokens.shape[0]
    gathered = lax.all_gather(tokens, "tp", axis=1, tiled=True)
    model_width = gathered.shape[1]
    ff_local = cotangent.shape[1]
    row_tiles = model_width // (tile_size * n_fsdp)
    col_tiles = ff_local // tile_size
    owner_tiles = row_tiles * col_tiles
    positions = jnp.arange(owner_tiles, dtype=jnp.int32)
    gate_table = gate_slots.reshape(n_fsdp, capacity)
    up_table = up_slots.reshape(n_fsdp, capacity)

    def selector(table, kind):
        picks = (table[:, :, None] == positions).astype(kind)
        return picks.reshape(table.shape[0], table.shape[1], row_tiles, col_tiles)

    gate_select = selector(gate_table, jnp.bfloat16)
    up_select = selector(up_table, jnp.bfloat16)
    gate_all, up_all = (
        lax.all_gather(gate_tiles, "fsdp", axis=0, tiled=True),
        lax.all_gather(up_tiles, "fsdp", axis=0, tiled=True),
    )

    def unpack(blocks, select):
        dense_tiles = jnp.einsum(
            "fcrj,fcab->frjab",
            select,
            blocks.reshape(n_fsdp, capacity, tile_size, tile_size),
            preferred_element_type=jnp.float32,
        )
        return dense_tiles.astype(jnp.bfloat16)

    w_gate = unpack(gate_all, gate_select)
    w_up = unpack(up_all, up_select)
    token_view = gathered.reshape(tok_rows, n_fsdp, row_tiles, tile_size)
    gate = jnp.einsum(
        "tfra,frjab->tjb", token_view, w_gate, preferred_element_type=jnp.float32
    ).reshape(tok_rows, ff_local)
    up = jnp.einsum(
        "tfra,frjab->tjb", token_view, w_up, preferred_element_type=jnp.float32
    ).reshape(tok_rows, ff_local)
    sigmoid_gate = jax.nn.sigmoid(gate)
    activated = gate * sigmoid_gate
    hidden = (activated * up).astype(jnp.bfloat16)
    upstream = cotangent.astype(jnp.float32)
    gate_grad = (upstream * up * sigmoid_gate * (1.0 + gate * (1.0 - sigmoid_gate))).astype(
        jnp.bfloat16
    )
    up_grad = (upstream * activated).astype(jnp.bfloat16)
    gate_view = gate_grad.reshape(tok_rows, col_tiles, tile_size)
    up_view = up_grad.reshape(tok_rows, col_tiles, tile_size)
    total = jnp.einsum(
        "frjab,tjb->frat", w_gate, gate_view, preferred_element_type=jnp.float32
    ) + jnp.einsum("frjab,tjb->frat", w_up, up_view, preferred_element_type=jnp.float32)
    input_part = lax.psum_scatter(
        total.reshape(model_width // n_tp * lax.axis_size("tp"), tok_rows).astype(jnp.bfloat16),
        "tp",
        scatter_dimension=0,
        tiled=True,
    ).astype(jnp.float32)
    input_grad = input_part.T.astype(jnp.bfloat16)
    gate_dense = jnp.einsum(
        "tfra,tjb->frajb", token_view, gate_view, preferred_element_type=jnp.float32
    ).astype(jnp.bfloat16)
    up_dense = jnp.einsum(
        "tfra,tjb->frajb", token_view, up_view, preferred_element_type=jnp.float32
    ).astype(jnp.bfloat16)
    gate_packed = jnp.einsum(
        "fcrj,frajb->fcab", gate_select, gate_dense, preferred_element_type=jnp.float32
    )
    up_packed = jnp.einsum(
        "fcrj,frajb->fcab", up_select, up_dense, preferred_element_type=jnp.float32
    )
    gate_packed = gate_packed.reshape(capacity * lax.axis_size("fsdp"), tile_size, tile_size)
    up_packed = up_packed.reshape(capacity * lax.axis_size("fsdp"), tile_size, tile_size)
    summed = lax.psum_scatter(
        jnp.concatenate([gate_packed, up_packed], axis=2).astype(jnp.bfloat16),
        "fsdp",
        scatter_dimension=0,
        tiled=True,
    ).astype(jnp.float32)
    gate_tile_grad = summed[:, :, :tile_size].astype(jnp.bfloat16)
    up_tile_grad = summed[:, :, tile_size:].astype(jnp.bfloat16)
    return (hidden, input_grad, gate_tile_grad, up_tile_grad)


def solution(mesh):
    placed = (
        P("fsdp", "tp"),
        P("fsdp", "tp", None),
        P("fsdp", "tp", None),
        P(None, "tp"),
        P(None, "tp"),
        P("fsdp", "tp"),
    )
    return jax.shard_map(
        per_device,
        mesh=mesh,
        in_specs=placed,
        out_specs=(P("fsdp", "tp"), P("fsdp", "tp"), P("fsdp", "tp", None), P("fsdp", "tp", None)),
        check_vma=False,
    )
```

profile of v0, /device:TPU:1, one launch (start us, length us, event | category | flops | bytes accessed | tf_op | source)
XLA Modules:
  0.0 511.9 jit_solution(2433849524178457601)
XLA Ops:
  7.2 0.0 all-gather.4.cloned.1.call-start
  7.2 0.7 all-gather.4.cloned.1.call-update
  7.9 0.0 all-gather.6.cloned.1.call-start
  7.9 1.8 copy.60
  9.7 0.0 all-gather.6.cloned.1.call-update
  9.8 0.0 all-gather.8.cloned.1.call-start
  9.8 0.7 all-gather.8.cloned.1.call-update
  10.5 0.0 reduce-scatter.5.cloned.1.call-start
  10.5 0.7 reduce
  11.2 0.7 reduce.1
  11.9 0.1 eq.49
  12.0 0.1 eq.42
  12.1 2.2 copy.67
  14.3 74.8 %all-gather.4.cloned.1.call-done = bf16[288,128,128]{2,1,0:T(8,128)(2,1)} async-done(((bf16[18,128,128]{2,1,0:T(8,128)(2,1)}), bf16[288,128,128]{2,1,0:T(8,128)(2,1)}) %all-gather.4.cloned.1.call-update) | async-done | bytes 9437200 | tf_op jit(solution)/shard_map/all_gather | solution.py:30
  89.1 15.7 %fusion.2 = bf16[16,2,14,128,128]{4,2,3,1,0:T(8,128)(2,1)} fusion(bf16[16,18,128,128,1]{3,2,1,0,4:T(8,128)(2,1)} %bitcast.119, s32[2,14]{1,0:T(2,128)S(1)} %multiply_add_fusion, s32[16,18]{1,0:T(8,128)S(1)} %eq.42), kind=kOutput, calls=%fused_computation.9 | convolution fusion | flops 264249216 | bytes 24118512 | tf_op jit(solution)/shard_map/fcrj,fcab->frjab/dot_general | solution.py:35
  104.9 11.7 %all-gather.6.cloned.1.call-done = bf16[256,4096]{0,1:T(8,128)(2,1)} async-done(((bf16[256,512]{0,1:T(8,128)(2,1)}), bf16[256,4096]{0,1:T(8,128)(2,1)}) %all-gather.6.cloned.1.call-update) | async-done | bytes 2097168 | tf_op jit(solution)/shard_map/all_gather | solution.py:13
  116.6 14.4 %fusion.6 = f32[14,128,256,1,1]{2,1,0,4,3:T(8,128)} fusion(bf16[256,16,2,128,1]{0,3,4,2,1:T(8,128)(2,1)} %bitcast.121, bf16[16,2,14,128,128]{4,2,3,1,0:T(8,128)(2,1)} %fusion.2), kind=kOutput, calls=%fused_computation.14 | convolution fusion | flops 3758096384 | bytes 18612224 | tf_op jit(solution)/shard_map/tfra,frjab->tjb/dot_general | solution.py:46
  131.0 63.4 %all-gather.8.cloned.1.call-done = bf16[288,128,128]{2,1,0:T(8,128)(2,1)} async-done(((bf16[18,128,128]{2,1,0:T(8,128)(2,1)}), bf16[288,128,128]{2,1,0:T(8,128)(2,1)}) %all-gather.8.cloned.1.call-update) | async-done | bytes 9437200 | tf_op jit(solution)/shard_map/all_gather | solution.py:31
  194.4 0.0 copy-start
  194.4 15.7 %fusion = bf16[16,2,14,128,128]{4,2,3,1,0:T(8,128)(2,1)} fusion(bf16[16,18,128,128,1]{3,2,1,0,4:T(8,128)(2,1)} %bitcast.120, s32[16,18]{1,0:T(8,128)S(1)} %eq.49, s32[2,14]{1,0:T(2,128)S(1)} %multiply_add_fusion), kind=kOutput, calls=%fused_computation.7 | convolution fusion | flops 264249216 | bytes 24118512 | tf_op jit(solution)/shard_map/fcrj,fcab->frjab/dot_general | solution.py:35
  210.1 0.0 copy-done
  210.1 0.0 copy-start.3
  210.1 0.0 copy-start.4
  210.1 13.6 %fusion.8 = f32[14,128,256,1,1]{2,1,0,4,3:T(8,128)S(1)} fusion(bf16[256,16,2,128,1]{0,3,4,2,1:T(8,128)(2,1)S(1)} %bitcast.122, bf16[16,2,14,128,128]{4,2,3,1,0:T(8,128)(2,1)} %fusion), kind=kOutput, calls=%fused_computation.16 | convolution fusion | flops 3758096384 | bytes 18612224 | tf_op jit(solution)/shard_map/tfra,frjab->tjb/dot_general | solution.py:49
  223.7 0.0 copy-done.3
  223.8 0.0 copy-done.4
  223.8 2.4 fusion.11
  226.1 7.2 %convert_bitcast_fusion = bf16[16,2,128,14,128]{2,4,1,0,3:T(8,128)(2,1)} fusion(bf16[256,14,128,1,1]{0,2,4,3,1:T(8,128)(2,1)S(1)} %bitcast.125, bf16[256,16,2,128,1]{0,3,2,1,4:T(8,128)(2,1)S(1)} %bitcast.123), kind=kOutput, calls=%fused_computation.5 | convolution fusion | flops 3765436416 | bytes 17694720 | tf_op jit(solution)/shard_map/tfra,tjb->frajb/dot_general | solution.py:75
  233.3 24.7 %copy.75 = bf16[16,2,128,14,128]{4,3,1,2,0:T(8,128)(2,1)} copy(bf16[16,2,128,14,128]{2,4,1,0,3:T(8,128)(2,1)} %convert_bitcast_fusion) | data formatting | bytes 29360128 | tf_op jit(solution)/shard_map/convert_element_type | solution.py:77
  258.0 10.2 %bitcast_convert_fusion = bf16[16,18,128,128]{3,1,2,0:T(8,128)(2,1)} fusion(bf16[16,2,128,14,128]{4,3,1,2,0:T(8,128)(2,1)} %copy.75, s32[16,18]{1,0:T(8,128)S(1)} %eq.49, s32[2,14]{1,0:T(2,128)S(1)} %multiply_add_fusion), kind=kOutput, calls=%fused_computation.2 | convolution fusion | flops 268967808 | bytes 24118512 | tf_op jit(solution)/shard_map/fcrj,frajb->fcab/dot_general | solution.py:81
  268.3 11.0 %copy.76 = bf16[16,18,128,128]{3,2,1,0:T(8,128)(2,1)} copy(bf16[16,18,128,128]{3,1,2,0:T(8,128)(2,1)} %bitcast_convert_fusion) | data formatting | bytes 18874368 | tf_op jit(solution)/shard_map/convert.4
  279.2 8.6 %convert_bitcast_fusion.1 = bf16[16,2,128,14,128]{2,4,1,0,3:T(8,128)(2,1)} fusion(bf16[256,14,128,1,1]{0,2,4,3,1:T(8,128)(2,1)} %bitcast.127, bf16[256,16,2,128,1]{0,3,2,1,4:T(8,128)(2,1)S(1)} %bitcast.124), kind=kOutput, calls=%fused_computation.6 | convolution fusion | flops 3765436416 | bytes 17694720 | tf_op jit(solution)/shard_map/tfra,tjb->frajb/dot_general | solution.py:72
  287.9 24.7 %copy.72 = bf16[16,2,128,14,128]{4,3,1,2,0:T(8,128)(2,1)} copy(bf16[16,2,128,14,128]{2,4,1,0,3:T(8,128)(2,1)} %convert_bitcast_fusion.1) | data formatting | bytes 29360128 | tf_op jit(solution)/shard_map/convert_element_type | solution.py:74
  312.6 10.4 %bitcast_convert_fusion.1 = bf16[16,18,128,128]{3,1,2,0:T(8,128)(2,1)} fusion(bf16[16,2,128,14,128]{4,3,1,2,0:T(8,128)(2,1)} %copy.72, s32[2,14]{1,0:T(2,128)S(1)} %multiply_add_fusion, s32[16,18]{1,0:T(8,128)S(1)} %eq.42), kind=kOutput, calls=%fused_computation.3 | convolution fusion | flops 268967808 | bytes 24118512 | tf_op jit(solution)/shard_map/fcrj,frajb->fcab/dot_general | solution.py:78
  323.0 11.0 %copy.73 = bf16[16,18,128,128]{3,2,1,0:T(8,128)(2,1)} copy(bf16[16,18,128,128]{3,1,2,0:T(8,128)(2,1)} %bitcast_convert_fusion.1) | data formatting | bytes 18874368 | tf_op jit(solution)/shard_map/convert.5
  334.0 16.8 %pad_maximum_fusion = bf16[288,128,256]{2,1,0:T(8,128)(2,1)} fusion(bf16[288,128,128]{2,1,0:T(8,128)(2,1)} %bitcast.117, bf16[288,128,128]{2,1,0:T(8,128)(2,1)} %bitcast.118), kind=kLoop, calls=%fused_computation.4 | loop fusion | flops 37748736 | bytes 37748736 | tf_op jit(solution)/shard_map/concatenate | solution.py:87
  350.8 0.0 copy-start.1
  350.8 0.0 reduce-scatter.5.cloned.1.call-update
  350.8 0.0 reduce-scatter.3.cloned.1.call-start
  350.9 1.1 copy-done.1
  352.0 9.3 %fusion.5 = f32[16,2,128,256,1]{3,2,4,1,0:T(8,128)S(1)} fusion(bf16[256,14,128,1,1]{0,2,1,4,3:T(8,128)(2,1)S(1)} %bitcast.128, bf16[16,2,14,128,128]{4,2,3,1,0:T(8,128)(2,1)} %fusion.2), kind=kOutput, calls=%fused_computation.13 | convolution fusion | flops 3758096384 | bytes 19791872 | tf_op jit(solution)/shard_map/frjab,tjb->frat/dot_general | solution.py:62
  361.3 0.0 copy-start.2
  361.3 10.7 %fusion.4 = bf16[16,2,128,256]{3,2,1,0:T(8,128)(2,1)} fusion(f32[16,2,128,256,1]{3,2,4,1,0:T(8,128)S(1)} %fusion.5, bf16[256,14,128,1,1]{0,2,1,4,3:T(8,128)(2,1)S(1)} %bitcast.126, bf16[16,2,14,128,128]{4,2,3,1,0:T(8,128)(2,1)} %fusion), kind=kOutput, calls=%fused_computation.12 | convolution fusion | flops 3760193536 | bytes 21889024 | tf_op jit(solution)/shard_map/frjab,tjb->frat/dot_general | solution.py:64
  372.0 4.2 copy.70
  376.1 0.0 reduce-scatter.3.cloned.1.call-update
  376.2 0.0 copy-done.2
  376.2 1.4 copy.77
  377.6 94.1 %reduce-scatter.5.cloned.1.call-done = bf16[18,128,256]{2,1,0:T(8,128)(2,1)} async-done(((bf16[288,128,256]{2,1,0:T(8,128)(2,1)}), bf16[18,128,256]{2,1,0:T(8,128)(2,1)}) %reduce-scatter.5.cloned.1.call-update) | async-done | bytes 1179664 | tf_op jit(solution)/shard_map/reduce_scatter | solution.py:86
  471.7 2.4 fusion.26
  474.1 30.8 %reduce-scatter.3.cloned.1.call-done = bf16[512,256]{0,1:T(8,128)(2,1)} async-done(((bf16[4096,256]{0,1:T(8,128)(2,1)}), bf16[512,256]{0,1:T(8,128)(2,1)}) %reduce-scatter.3.cloned.1.call-update) | async-done | bytes 262160 | tf_op jit(solution)/shard_map/reduce_scatter | solution.py:65
  (1 shorter events, 0.0 us)
Async XLA Ops:
  7.2 82.0 %all-gather.4.cloned.1.call-start = ((), (), s32[]{:S(2)}) async-start(), calls=%async_computation.2 | async-start | bytes 10027008 | tf_op jit(solution)/shard_map/all_gather | solution.py:30
  7.9 108.7 %all-gather.6.cloned.1.call-start = ((), (), s32[]{:S(2)}) async-start(), calls=%async_computation.3 | async-start | bytes 2359296 | tf_op jit(solution)/shard_map/all_gather | solution.py:13
  9.8 184.6 %all-gather.8.cloned.1.call-start = ((), (), s32[]{:S(2)}) async-start(), calls=%async_computation.4 | async-start | bytes 10027008 | tf_op jit(solution)/shard_map/all_gather | solution.py:31
  10.5 461.2 %reduce-scatter.5.cloned.1.call-start = ((), (), s32[]{:S(2)}) async-start(), calls=%async_computation.6 | async-start | bytes 20054016 | tf_op jit(solution)/shard_map/reduce_scatter | solution.py:86
  194.4 15.7 %copy-start = (bf16[256,4096]{0,1:T(8,128)(2,1)S(1)}, bf16[256,4096]{0,1:T(8,128)(2,1)}, u32[]{:S(2)}) copy-start(bf16[256,4096]{0,1:T(8,128)(2,1)} %all-gather.6.cloned.1.call-done) | copy-start | bytes 6291460
  210.1 13.6 %copy-start.3 = (bf16[256,1792]{0,1:T(8,128)(2,1)S(1)}, bf16[256,1792]{0,1:T(8,128)(2,1)}, u32[]{:S(2)}) copy-start(bf16[256,1792]{0,1:T(8,128)(2,1)} %copy.67) | copy-start | bytes 2752516
  210.1 13.6 %copy-start.4 = (f32[14,128,256,1,1]{2,1,0,4,3:T(8,128)S(1)}, f32[14,128,256,1,1]{2,1,0,4,3:T(8,128)}, u32[]{:S(2)}) copy-start(f32[14,128,256,1,1]{2,1,0,4,3:T(8,128)} %fusion.6) | copy-start | bytes 5505028
  350.8 1.2 copy-start.1
  350.8 154.1 %reduce-scatter.3.cloned.1.call-start = ((), (), s32[]{:S(2)}) async-start(), calls=%async_computation.5 | async-start | bytes 2359296 | tf_op jit(solution)/shard_map/reduce_scatter | solution.py:65
  361.3 14.9 %copy-start.2 = (bf16[256,1792]{0,1:T(8,128)(2,1)S(1)}, bf16[256,1792]{0,1:T(8,128)(2,1)}, u32[]{:S(2)}) copy-start(bf16[256,1792]{0,1:T(8,128)(2,1)} %get-tuple-element.17) | copy-start | bytes 2752516
Sparse Core Ops, SparseCore 0:
  10.2 78.8 all-gather.3
  91.4 25.1 all-gather.5
  118.8 75.5 all-gather.7
  350.9 120.6 reduce-scatter.4
  474.5 30.3 reduce-scatter.2
where the time goes:
time: 520 us; the launch traced here: 512 us
  waiting for transfers between devices  276 us (53%)
  matrix products  116 us (22%)
  local copies, waits for them, and re-layouts  84.6 us (16%)
  other arithmetic  20.6 us (4%)
  between operations  14.3 us (3%)
    reduce_scatter x1, waiting for transfers between devices, per_device(): lax.psum_scatter(jnp.concatenate([gate_packed, up_packed], axis=2).astype...  94.1 us
    all_gather x1, waiting for transfers between devices, per_device(): lax.all_gather(gate_tiles, 'fsdp', axis=0, tiled=True)  74.8 us
    all_gather x1, waiting for transfers between devices, per_device(): lax.all_gather(up_tiles, 'fsdp', axis=0, tiled=True)  63.4 us
    dot_general x2, matrix products, unpack(): jnp.einsum('fcrj,fcab->frjab', select, blocks.reshape(n_fsdp, capacity, t...  31.5 us
    reduce_scatter x1, waiting for transfers between devices, per_device(): lax.psum_scatter(total.reshape(model_width // n_tp * lax.axis_size('tp'),...  30.8 us
    convert_element_type x1, local copies, waits for them, and re-layouts, per_device(): up_dense = jnp.einsum('tfra,tjb->frajb', token_view, up_view, preferred_e...  24.7 us
    convert_element_type x1, local copies, waits for them, and re-layouts, per_device(): gate_dense = jnp.einsum('tfra,tjb->frajb', token_view, gate_view, preferr...  24.7 us
    another operation x2, local copies, waits for them, and re-layouts  21.9 us
  transfers between devices with their start and end apart: 5, of which 5 were waited for; matrix products, arithmetic and copies ran while one was open for 12% of the time, Pallas kernels for 0%

commit v1 on v0

v1 whole, which is shorter than its diff:
```python
import functools

import jax
import jax.numpy as jnp
from jax import lax
from jax.experimental import pallas as pl
from jax.experimental.pallas import tpu as pltpu
from jax.sharding import Mesh
from jax.sharding import PartitionSpec as P

RING = 4
TILE = 128
CAP = 18
HALF = CAP // 2
ROW_TILES = 2
COL_TILES = 14
TOK = 256
ROWS = ROW_TILES * TILE
FF = COL_TILES * TILE
ALL = RING * 256
STEP = 256
F32 = jnp.float32
BF16 = jnp.bfloat16
PARAMS = pltpu.CompilerParams(vmem_limit_bytes=40 * 2**20)


def shift(value, axis, by):
    return lax.ppermute(value, axis, [(i, (i + by) % RING) for i in range(RING)])


def gather_ring(value, axis):
    half = value.shape[0] // 2
    below = shift(value, axis, 1)
    above = shift(value, axis, -1)
    far_low = shift(below[:half], axis, 1)
    far_high = shift(above[half:], axis, -1)
    return value, below, above, far_low, far_high


def add(a, b):
    return (a.astype(F32) + b.astype(F32)).astype(BF16)


def scatter_ring(own, to_next, far_low, far_high, to_last, axis):
    half = far_low.shape[0]
    low = shift(far_low, axis, 1)
    high = shift(far_high, axis, -1)
    to_next = jnp.concatenate([add(to_next[:half], low), to_next[half:]], 0)
    to_last = jnp.concatenate([to_last[:half], add(to_last[half:], high)], 0)
    return own, shift(to_next, axis, 1), shift(to_last, axis, -1)


def swap_core(value):
    return lax.ppermute(value, "core", [(0, 1), (1, 0)])


def mod(value):
    return lax.rem(value + 2 * RING, RING)


def place_of(meta):
    return meta[0], meta[1], meta[2], meta[3]


def owner_base(kind, meta, distance):
    y, z, _, _ = place_of(meta)
    owner = mod(y + distance) * RING + z if kind == "gate" else y * RING + mod(z + distance)
    return owner * CAP


def fill_weights(kind, meta, slots, pieces, dense, position):
    dense[...] = jnp.zeros(dense.shape, dense.dtype)
    own, below, above, far_low, far_high = pieces
    for piece, distance, first, count in (
        (own, 0, 0, CAP),
        (below, 3, 0, CAP),
        (above, 1, 0, CAP),
        (far_low, 2, 0, HALF),
        (far_high, 2, HALF, HALF),
    ):
        base = owner_base(kind, meta, distance) + first
        row_base = position(distance) * ROWS

        def put(index, _, piece=piece, base=base, row_base=row_base):
            spot = slots[base + index]

            @pl.when(spot >= 0)
            def _():
                row = pl.multiple_of(row_base + lax.div(spot, COL_TILES) * TILE, TILE)
                col = pl.multiple_of(lax.rem(spot, COL_TILES) * TILE, TILE)
                dense[pl.ds(row, TILE), pl.ds(col, TILE)] = piece[index]

            return 0

        lax.fori_loop(0, count, put, 0)


def token_places(kind, meta):
    y, z, x, c = place_of(meta)
    places = []
    for core in (c, 1 - c):
        if kind == "gate":
            row = 2 * core * TOK
            for step, first, count in ((0, 0, 512), (-1, 0, 512), (1, 0, 512), (2, 0, 256), (2, 256, 256)):
                col = mod(x + step - y) * ROWS
                places.append(((0, count, 0, 256, row + first, col),))
        else:
            cols = [mod(2 * core + b - z) * ROWS for b in range(2)]
            for step, first, count in ((0, 0, 256), (-1, 0, 256), (1, 0, 256), (2, 0, 128), (2, 128, 128)):
                row = mod(x + step - y) * TOK + first
                places.append(tuple((0, count, 256 * b, 256, row, cols[b]) for b in range(2)))
    return places


def forward_kernel(kind, meta, slots, *refs):
    tokens, tiles = refs[:10], refs[10:15]
    own, to_next, far_low, far_high, to_last, together, dense = refs[15:]
    step = pl.program_id(0)

    @pl.when(step == 0)
    def _():
        fill_weights(kind, meta, slots, tiles, dense, lambda distance: distance)
        for ref, blocks in zip(tokens, token_places(kind, meta)):
            for row, rows, col, cols, to_row, to_col in blocks:
                together[
                    pl.ds(pl.multiple_of(to_row, TILE), rows),
                    pl.ds(pl.multiple_of(to_col, TILE), cols),
                ] = ref[row : row + rows, col : col + cols]

    weights = dense[:, pl.ds(pl.multiple_of(step * STEP, STEP), STEP)]
    share = jnp.dot(together[...], weights, preferred_element_type=F32).astype(BF16)
    own[...] = share[:TOK]
    to_next[...] = share[TOK : 2 * TOK]
    far_low[...] = share[2 * TOK : 2 * TOK + TOK // 2]
    far_high[...] = share[2 * TOK + TOK // 2 : 3 * TOK]
    to_last[...] = share[3 * TOK :]


def whole(shape):
    return pl.BlockSpec(shape, lambda *_: (0,) * len(shape))


def columns(rows):
    return pl.BlockSpec((rows, STEP), lambda i, *_: (0, i))


def forward(kind, meta, slots, tokens, tiles):
    rows = (TOK, TOK, TOK // 2, TOK // 2, TOK)
    return pl.pallas_call(
        functools.partial(forward_kernel, kind),
        grid_spec=pltpu.PrefetchScalarGridSpec(
            num_scalar_prefetch=2,
            grid=(FF // STEP,),
            in_specs=[whole(a.shape) for a in (*tokens, *tiles)],
            out_specs=[columns(n) for n in rows] + [whole((ALL, ALL))],
            scratch_shapes=[pltpu.VMEM((ALL, FF), BF16)],
        ),
        out_shape=[jax.ShapeDtypeStruct((n, FF), BF16) for n in rows]
        + [jax.ShapeDtypeStruct((ALL, ALL), BF16)],
        compiler_params=PARAMS,
        cost_estimate=pl.CostEstimate(flops=2 * ALL * ALL * FF, bytes_accessed=12 * 2**20, transcendentals=0),
        name=kind + "_forward",
    )(meta, slots, *tokens, *tiles)


def middle_kernel(g0, g1, g2, u0, u1, u2, cot, hidden, gate_grad, up_grad):
    gate = g0[...].astype(F32) + g1[...].astype(F32) + g2[...].astype(F32)
    up = u0[...].astype(F32) + u1[...].astype(F32) + u2[...].astype(F32)
    upstream = cot[...].astype(F32)
    sigmoid = jax.nn.sigmoid(gate)
    activated = gate * sigmoid
    hidden[...] = (activated * up).astype(BF16)
    gate_grad[...] = (upstream * up * sigmoid * (1.0 + gate * (1.0 - sigmoid))).astype(BF16)
    up_grad[...] = (upstream * activated).astype(BF16)


def middle(gate_terms, up_terms, cotangent):
    return pl.pallas_call(
        middle_kernel,
        grid=(FF // STEP,),
        in_specs=[columns(TOK)] * 7,
        out_specs=[columns(TOK)] * 3,
        out_shape=[jax.ShapeDtypeStruct((TOK, FF), BF16)] * 3,
        compiler_params=PARAMS,
        cost_estimate=pl.CostEstimate(flops=TOK * FF * 20, bytes_accessed=10 * TOK * FF * 2, transcendentals=TOK * FF),
        name="middle",
    )(*gate_terms, *up_terms, cotangent)


def tile_grad_kernel(kind, meta, slots, turned, own, below, above, far_low, far_high, o0, o1, o2a, o2b, o3, grads, slot_of):
    step = pl.program_id(0)

    @pl.when(step == 0)
    def _():
        for ref in (o0, o1, o2a, o2b, o3):
            ref[...] = jnp.zeros(ref.shape, ref.dtype)
        for distance in range(RING):
            base = owner_base(kind, meta, distance)
            for spot in range(ROW_TILES * COL_TILES):
                slot_of[distance * ROW_TILES * COL_TILES + spot] = -1

            def note(index, _, base=base, distance=distance):
                spot = slots[base + index]

                @pl.when(spot >= 0)
                def _():
                    slot_of[distance * ROW_TILES * COL_TILES + spot] = index

                return 0

            lax.fori_loop(0, CAP, note, 0)

    grads[0:TOK] = own[...]
    grads[TOK : 2 * TOK] = above[...]
    grads[2 * TOK : 2 * TOK + TOK // 2] = far_low[...]
    grads[2 * TOK + TOK // 2 : 3 * TOK] = far_high[...]
    grads[3 * TOK :] = below[...]
    for distance in range(RING):
        share = jnp.dot(
            turned[distance * ROWS : (distance + 1) * ROWS], grads[...], preferred_element_type=F32
        ).astype(BF16)
        for r in range(ROW_TILES):
            for b in range(STEP // TILE):
                slot = slot_of[(distance * ROW_TILES + r) * COL_TILES + step * (STEP // TILE) + b]
                tile = share[r * TILE : (r + 1) * TILE, b * TILE : (b + 1) * TILE]
                if distance == 2:

                    @pl.when((slot >= 0) & (slot < HALF))
                    def _(slot=slot, tile=tile):
                        o2a[slot] = tile

                    @pl.when(slot >= HALF)
                    def _(slot=slot, tile=tile):
                        o2b[slot - HALF] = tile

                else:
                    out = (o0, o1, None, o3)[distance]

                    @pl.when(slot >= 0)
                    def _(slot=slot, tile=tile, out=out):
                        out[slot] = tile


def tile_grad(kind, meta, slots, turned, pieces):
    shapes = [(n, TILE, TILE) for n in (CAP, CAP, HALF, HALF, CAP)]
    return pl.pallas_call(
        functools.partial(tile_grad_kernel, kind),
        grid_spec=pltpu.PrefetchScalarGridSpec(
            num_scalar_prefetch=2,
            grid=(FF // STEP,),
            in_specs=[whole((ALL, ALL))] + [columns(a.shape[0]) for a in pieces],
            out_specs=[whole(s) for s in shapes],
            scratch_shapes=[
                pltpu.VMEM((ALL, STEP), BF16),
                pltpu.SMEM((RING * ROW_TILES * COL_TILES,), jnp.int32),
            ],
        ),
        out_shape=[jax.ShapeDtypeStruct(s, BF16) for s in shapes],
        compiler_params=PARAMS,
        cost_estimate=pl.CostEstimate(flops=2 * ALL * ALL * FF, bytes_accessed=9 * 2**20, transcendentals=0),
        name=kind + "_tile_grad",
    )(meta, slots, turned, *pieces)


def input_grad_kernel(kind, meta, slots, *refs):
    tiles, pieces = refs[:5], refs[5:10]
    keep, give, dense, grads = refs[10:]
    y, z, x, c = place_of(meta)
    step = pl.program_id(0)
    by_x = lambda distance: mod(y + distance - x)

    @pl.when(step == 0)
    def _():
        if kind == "gate":
            weight_place, token_place = by_x, lambda distance: mod(distance - 2 * c)
        else:
            weight_place, token_place = (lambda distance: mod(z + distance - 2 * c)), by_x
        fill_weights(kind, meta, slots, tiles, dense, weight_place)
        for ref, distance, first in zip(pieces, (0, 3, 1, 2, 2), (0, 0, 0, 0, TOK // 2)):
            row = pl.multiple_of(token_place(distance) * TOK + first, TILE)
            grads[pl.ds(row, ref.shape[0]), :] = ref[...]

    here = pl.ds(pl.multiple_of(step * 256, 256), 256)
    contract = (((1,), (1,)), ((), ()))
    if kind == "gate":
        share = lax.dot_general(grads[...], dense[here, :], contract, preferred_element_type=F32).astype(BF16)
        keep[0] = share[: ALL // 2]
        give[0] = share[ALL // 2 :]
    else:
        share = lax.dot_general(grads[here, :], dense[...], contract, preferred_element_type=F32).astype(BF16)
        keep[0] = share[:, : ALL // 2]
        give[0] = share[:, ALL // 2 :]


def input_grad(kind, meta, slots, tiles, pieces):
    shape = (RING, 512, 256) if kind == "gate" else (RING, 256, 512)
    block = pl.BlockSpec((1, *shape[1:]), lambda i, *_: (i, 0, 0))
    return pl.pallas_call(
        functools.partial(input_grad_kernel, kind),
        grid_spec=pltpu.PrefetchScalarGridSpec(
            num_scalar_prefetch=2,
            grid=(RING,),
            in_specs=[whole(a.shape) for a in (*tiles, *pieces)],
            out_specs=[block, block],
            scratch_shapes=[pltpu.VMEM((ALL, FF), BF16), pltpu.VMEM((ALL, FF), BF16)],
        ),
        out_shape=[jax.ShapeDtypeStruct(shape, BF16)] * 2,
        compiler_params=PARAMS,
        cost_estimate=pl.CostEstimate(flops=2 * ALL * ALL * FF, bytes_accessed=8 * 2**20, transcendentals=0),
        name=kind + "_input_grad",
    )(meta, slots, *tiles, *pieces)


def exchange_pairs(parity):
    pairs = []
    for z in range(RING):
        for c in range(2):
            to_z = 2 * c + (z + parity) % 2
            pairs.append((z * 2 + c, to_z * 2 + ((z - to_z) % RING) // 2))
    return pairs


TURN = [(y * RING + x, x * RING + y) for y in range(RING) for x in range(RING)]


def per_device(tokens, gate_tiles, up_tiles, gate_slots, up_slots, cotangent):
    y, z, x, c = (lax.axis_index(a) for a in ("y", "z", "x", "core"))
    meta = jnp.stack([y, z, x, c]).astype(jnp.int32)
    gate_slots = gate_slots.reshape(-1)
    up_slots = up_slots.reshape(-1)

    low, high = tokens[:, :256], tokens[:, 256:]
    odd = z % 2 == 1
    even_block = lax.ppermute(jnp.where(odd, high, low), ("z", "core"), exchange_pairs(0))
    odd_block = lax.ppermute(jnp.where(odd, low, high), ("z", "core"), exchange_pairs(1))
    turned = lax.ppermute(tokens, ("y", "x"), TURN)
    gate_pieces = gather_ring(gate_tiles, "y")
    up_pieces = gather_ring(up_tiles, "z")
    gate_tokens = gather_ring(jnp.concatenate([even_block, odd_block], 0), "x")
    up_tokens = gather_ring(turned, "x")
    gate_tokens = gate_tokens + tuple(swap_core(a) for a in gate_tokens)
    up_tokens = up_tokens + tuple(swap_core(a) for a in up_tokens)

    *gate_shares, gate_x = forward("gate", meta, gate_slots, gate_tokens, gate_pieces)
    *up_shares, up_x = forward("up", meta, up_slots, up_tokens, up_pieces)
    gate_terms = scatter_ring(*gate_shares, "z")
    up_terms = scatter_ring(*up_shares, "y")
    hidden, gate_grad, up_grad = middle(gate_terms, up_terms, cotangent)

    gate_grads = gather_ring(gate_grad, "z")
    up_grads = gather_ring(up_grad, "y")
    gate_sums = tile_grad("gate", meta, gate_slots, gate_x.T, gate_grads)
    up_sums = tile_grad("up", meta, up_slots, up_x.T, up_grads)
    gate_out = scatter_ring(*gate_sums, "y")
    up_out = scatter_ring(*up_sums, "z")

    def total(terms):
        return terms[0].astype(F32) + terms[1].astype(F32) + terms[2].astype(F32)

    parts = []
    for kind, slots, tiles, grads in (
        ("gate", gate_slots, gate_pieces, gate_grads),
        ("up", up_slots, up_pieces, up_grads),
    ):
        keep, give = input_grad(kind, meta, slots, tiles, grads)
        both = add(keep, swap_core(give))
        half = both.shape[1] // 2
        parts.append(total(scatter_ring(both[0], both[1], both[2, :half], both[2, half:], both[3], "x")).astype(BF16))
    gate_part, up_part = parts
    even_block, odd_block = (
        lax.ppermute(gate_part[256 * j : 256 * (j + 1)], ("z", "core"), [(b, a) for a, b in exchange_pairs(j)])
        for j in range(2)
    )
    low, high = jnp.where(odd, odd_block, even_block), jnp.where(odd, even_block, odd_block)
    up_part = lax.ppermute(up_part, ("y", "x"), TURN)
    input_sum = add(jnp.concatenate([low, high], 1), up_part)
    return hidden, input_sum, total(gate_out).astype(BF16), total(up_out).astype(BF16)


def solution(mesh):
    grid = Mesh(mesh.devices.reshape(RING, RING, RING, 2), ("y", "z", "x", "core"))
    rows, cols = ("y", "z"), ("x", "core")
    placed = (
        P(rows, cols),
        P(rows, cols, None),
        P(rows, cols, None),
        P(None, cols),
        P(None, cols),
        P(rows, cols),
    )
    return jax.shard_map(
        per_device,
        mesh=grid,
        in_specs=placed,
        out_specs=(P(rows, cols), P(rows, cols), P(rows, cols, None), P(rows, cols, None)),
        check_vma=False,
    )
```

time: 520 us -> 329 us (0.63)
  waiting for transfers between devices: 276 us -> 74.4 us
  matrix products: 116 us -> 0 us
  starting transfers between devices: 0.2 us -> 115 us
  Pallas kernels: 0 us -> 70.5 us
  local copies, waits for them, and re-layouts: 84.6 us -> 53.8 us
  other arithmetic: 20.6 us -> 7.4 us
  between operations: 14.3 us -> 1.77 us
    all_gather x3 -> x0, waiting for transfers between devices: 150 us -> none  [the longest x1 74.8 us: per_device(): lax.all_gather(gate_tiles, 'fsdp', axis=0, tiled=True)]
    reduce_scatter x2 -> x0, waiting for transfers between devices: 125 us -> none  [the longest x1 94.1 us: per_device(): lax.psum_scatter(jnp.concatenate([gate_packed, up_packed], axis=2).astype...]
    dot_general x10 -> x0, matrix products: 116 us -> none  [the longest x2 31.5 us: unpack(): jnp.einsum('fcrj,fcab->frjab', select, blocks.reshape(n_fsdp, capacity, t...]
    ppermute x0 -> x66, starting transfers between devices: none -> 115 us  [the longest x48 67.6 us: shift(): lax.ppermute(value, axis, [(i, (i + by) % RING) for i in range(RING)])]
    ppermute x0 -> x66, waiting for transfers between devices: none -> 74.4 us  [the longest x48 70.3 us: shift(): lax.ppermute(value, axis, [(i, (i + by) % RING) for i in range(RING)])]
    pallas_call x0 -> x7, Pallas kernels: none -> 70.5 us  [the longest x2 30.7 us: tile_grad(): pl.pallas_call(functools.partial(tile_grad_kernel, kind), grid_spec=pltpu...]
    convert_element_type x3 -> x0, local copies, waits for them, and re-layouts: 53.6 us -> none  [the longest x1 24.7 us: per_device(): up_dense = jnp.einsum('tfra,tjb->frajb', token_view, up_view, preferred_e...]
    unnamed x13 -> x141, local copies, waits for them, and re-layouts: 6.5 us -> 37.5 us
  transfers between devices with their start and end apart: 5 -> 66, of which waited for: 5 -> 18; matrix products, arithmetic and copies ran while one was open for 12% -> 7% of each run, Pallas kernels for 0% -> 21%
where the time goes in v1:
time: 329 us; the launch traced here: 323 us
  starting transfers between devices  115 us (35%)
  waiting for transfers between devices  74.4 us (23%)
  Pallas kernels  70.5 us (21%)
  local copies, waits for them, and re-layouts  53.8 us (16%)
  other arithmetic  7.4 us (2%)
    ppermute x48, waiting for transfers between devices, shift(): lax.ppermute(value, axis, [(i, (i + by) % RING) for i in range(RING)])  70.3 us
    ppermute x48, starting transfers between devices, shift(): lax.ppermute(value, axis, [(i, (i + by) % RING) for i in range(RING)])  67.6 us
    unnamed x141, local copies, waits for them, and re-layouts  37.5 us
    pallas_call x2, Pallas kernels, tile_grad(): pl.pallas_call(functools.partial(tile_grad_kernel, kind), grid_spec=pltpu...  30.7 us
    ppermute x12, starting transfers between devices, swap_core(): return lax.ppermute(value, 'core', [(0, 1), (1, 0)])  22.1 us
    pallas_call x2, Pallas kernels, forward(): pl.pallas_call(functools.partial(forward_kernel, kind), grid_spec=pltpu.P...  18.7 us
    pallas_call x2, Pallas kernels, input_grad(): pl.pallas_call(functools.partial(input_grad_kernel, kind), grid_spec=pltp...  17.7 us
    ppermute x2, starting transfers between devices, per_device(): lax.ppermute(gate_part[256 * j:256 * (j + 1)], ('z', 'core'), [(b, a) for...  16.1 us
  transfers between devices with their start and end apart: 66, of which 18 were waited for; matrix products, arithmetic and copies ran while one was open for 7% of the time, Pallas kernels for 21%

profile of v1, /device:TPU:1, one launch (start us, length us, event | category | flops | bytes accessed | tf_op | source)
XLA Modules:
  0.0 323.1 jit_solution(10662641902643500238)
XLA Ops:
  1.6 6.3 %collective-permute-start = (bf16[256,256]{1,0:T(8,128)(2,1)S(1)}, bf16[256,256]{1,0:T(8,128)(2,1)S(1)}, u32[]{:S(2)}, u32[]{:S(2)}) collective-permute-start(bf16[256,256]{1,0:T(8,128)(2,1)S(1)} %get-tuple-element.79), channel_id=1, source_target_pairs={{0,0},{1,17},{8,8},{9,25},{16,1},{17,16},{24,9},{25,24},{2,2},{3,1... | collective-permute-start | bytes 393224 | tf_op jit(solution)/shard_map/ppermute | solution.py:334
  8.8 1.6 collective-permute-start.19
  11.3 2.3 collective-permute-done.1
  13.7 1.3 collective-permute-start.2
  15.0 1.5 collective-permute-start.3
  17.0 1.5 collective-permute-start.11
  18.5 11.8 %collective-permute-start.12 = (bf16[18,128,128]{2,1,0:T(8,128)(2,1)}, bf16[18,128,128]{2,1,0:T(8,128)(2,1)S(1)}, u32[]{:S(2)}, u32[]{:S(2)}) collective-permute-start(bf16[18,128,128]{2,1,0:T(8,128)(2,1)} %refs_0_.2), channel_id=1, source_target_pairs={{0,96},{32,0},{64,32},{96,64},{1,97},{33,1},{65,33},{97,65},{2,98}... | collective-permute-start | bytes 1769480 | tf_op jit(solution)/shard_map/ppermute | solution.py:28
  30.3 3.2 collective-permute-done.2.refs_1_
  34.4 2.7 collective-permute-start.5
  37.1 7.4 %collective-permute-done.4.refs_3_ = bf16[256,256]{1,0:T(8,128)(2,1)S(1)} collective-permute-done((bf16[256,256]{1,0:T(8,128)(2,1)S(1)}, bf16[256,256]{1,0:T(8,128)(2,1)S(1)}, u32[]{:S(2)}, u32[]{:S(2)}) %collective-permute-start.4) | collective-permute-done | bytes 131104 | tf_op jit(solution)/shard_map/ppermute | solution.py:28
  44.4 2.7 collective-permute-start.30
  47.1 5.5 %collective-permute-done.21.refs_2_ = bf16[256,512]{1,0:T(8,128)(2,1)} collective-permute-done((bf16[256,512]{1,0:T(8,128)(2,1)S(1)}, bf16[256,512]{1,0:T(8,128)(2,1)}, u32[]{:S(2)}, u32[]{:S(2)}) %collective-permute-start.21) | collective-permute-done | bytes 262176 | tf_op jit(solution)/shard_map/ppermute | solution.py:28
  52.6 3.4 %collective-permute-start.24 = (bf16[256,512]{1,0:T(8,128)(2,1)S(1)}, bf16[256,512]{1,0:T(8,128)(2,1)S(1)}, u32[]{:S(2)}, u32[]{:S(2)}) collective-permute-start(bf16[256,512]{1,0:T(8,128)(2,1)S(1)} %collective-permute-done.19.refs_0_), channel_id=1, source_target_pairs={{0,1},{1,0},{2,3},{3,2},{4,5},{5,4},{6,7},{7,6},{8,9},{9,8},{10,11... | collective-permute-start | bytes 786440 | tf_op jit(solution)/shard_map/ppermute | solution.py:54
  60.2 2.7 collective-permute-start.14
  66.9 1.6 slice.221
  69.8 2.7 collective-permute-start.23
  74.0 1.7 collective-permute-done.22.refs_3_
  77.3 2.7 collective-permute-start.32
  82.0 1.1 copy-done.15
  83.0 1.1 copy-done.18
  86.0 1.1 copy-done.37
  95.4 9.1 %gate_forward.1 = (bf16[256,1792]{1,0:T(8,128)(2,1)S(1)}, bf16[256,1792]{1,0:T(8,128)(2,1)S(1)}, bf16[128,1792]{1,0:T(8,128)(2,1)}, bf16[128,1792]{1,0:T(8,128)(...) custom-call(s32[4]{0:T(128)S(1)} %pad_add_fusion.meta, s32[288]{0:T(512)S(1)} %reduce.slots, ...), custom_call_target="tpu_custom_call" | custom-call | flops 3758096384 | bytes 12582912 | tf_op jit(solution)/shard_map/gate_forward/pallas_call | solution.py:149
  107.9 1.2 slice.173
  110.1 3.0 collective-permute-start.17
  117.0 9.6 %up_forward.1 = (bf16[256,1792]{1,0:T(8,128)(2,1)S(1)}, bf16[256,1792]{1,0:T(8,128)(2,1)S(1)}, bf16[128,1792]{1,0:T(8,128)(2,1)S(1)}, bf16[128,1792]{1,0:T(8,128...) custom-call(s32[4]{0:T(128)S(1)} %pad_add_fusion.meta, s32[288]{0:T(512)S(1)} %reduce.1.slots, ...), custom_call_target="tpu_custom_call" | custom-call | flops 3758096384 | bytes 12582912 | tf_op jit(solution)/shard_map/up_forward/pallas_call | solution.py:149
  126.8 2.7 collective-permute-start.35
  129.5 1.2 add_convert_fusion.7
  131.1 2.7 collective-permute-start.18
  133.8 5.1 %collective-permute-done.33 = bf16[128,1792]{1,0:T(8,128)(2,1)S(1)} collective-permute-done((bf16[128,1792]{1,0:T(8,128)(2,1)S(1)}, bf16[128,1792]{1,0:T(8,128)(2,1)S(1)}, u32[]{:S(2)}, u32[]{:S(2)}) %collective-permute-start.33) | collective-permute-done | bytes 458784 | tf_op jit(solution)/shard_map/ppermute | solution.py:28
  139.3 2.7 collective-permute-start.36
  142.0 10.2 %collective-permute-done.16.g1 = bf16[256,1792]{1,0:T(8,128)(2,1)S(1)} collective-permute-done((bf16[256,1792]{1,0:T(8,128)(2,1)S(1)}, bf16[256,1792]{1,0:T(8,128)(2,1)S(1)}, u32[]{:S(2)}, u32[]{:S(2)}) %collective-permute-start.16) | collective-permute-done | bytes 917536 | tf_op jit(solution)/shard_map/ppermute | solution.py:28
  152.2 7.9 %collective-permute-done.34.u1 = bf16[256,1792]{1,0:T(8,128)(2,1)S(1)} collective-permute-done((bf16[256,1792]{1,0:T(8,128)(2,1)S(1)}, bf16[256,1792]{1,0:T(8,128)(2,1)S(1)}, u32[]{:S(2)}, u32[]{:S(2)}) %collective-permute-start.34) | collective-permute-done | bytes 917536 | tf_op jit(solution)/shard_map/ppermute | solution.py:28
  160.1 3.4 %middle.1 = (bf16[256,1792]{1,0:T(8,128)(2,1)}, bf16[256,1792]{1,0:T(8,128)(2,1)S(1)}, bf16[256,1792]{1,0:T(8,128)(2,1)S(1)}) custom-call(bf16[256,1792]{1,0:T(8,128)(2,1)S(1)} %get-tuple-element.33.g0, bf16[256,1792]{1,0:T(8,128)(2,1)S(1)} %collective-permute-done.16.g1, bf16[256,1792]{1,0:T(8,128)(2,1)S(1)} %collective-permute-done.18.g2, ...), custom_call_target="tpu_custom_call" | custom-call | flops 9175040 | bytes 9175040 | tf_op jit(solution)/shard_map/middle/pallas_call | solution.py:178
  163.6 2.7 collective-permute-start.49
  166.3 2.7 collective-permute-start.38
  169.0 14.7 %collective-permute-done.48.refs_6_.below = bf16[256,1792]{1,0:T(8,128)(2,1)S(1)} collective-permute-done((bf16[256,1792]{1,0:T(8,128)(2,1)S(1)}, bf16[256,1792]{1,0:T(8,128)(2,1)S(1)}, u32[]{:S(2)}, u32[]{:S(2)}) %collective-permute-start.48) | collective-permute-done | bytes 917536 | tf_op jit(solution)/shard_map/ppermute | solution.py:28
  186.2 2.7 collective-permute-start.51
  192.4 2.7 collective-permute-start.40
  195.1 2.6 copy.10
  197.7 2.9 copy.11
  200.6 1.2 copy-done.8
  201.7 1.1 copy-done.22
  202.8 1.1 copy-done.25
  203.9 1.2 copy-done.31
  206.2 9.0 %up_input_grad.1 = (bf16[4,256,512]{2,1,0:T(8,128)(2,1)S(1)}, bf16[4,256,512]{2,1,0:T(8,128)(2,1)S(1)}) custom-call(s32[4]{0:T(128)S(1)} %pad_add_fusion.meta, s32[288]{0:T(512)S(1)} %reduce.1.slots, bf16[18,128,128]{2,1,0:T(8,128)(2,1)S(1)} %copy-done.36, bf16[18,128,128]{2,1,0:T(8,128)(2,1)S(1)} %copy-done.22, bf16[18,128,128]{2,1,0:T(8,128)(2,1)S(1)} %copy-done.25, ...), custom_call_target="tpu_custom_call" | custom-call | flops 3758096384 | bytes 8388608 | tf_op jit(solution)/shard_map/up_input_grad/pallas_call | solution.py:298
  215.2 14.9 %collective-permute-start.52 = (bf16[4,256,512]{2,1,0:T(8,128)(2,1)S(1)}, bf16[4,256,512]{2,1,0:T(8,128)(2,1)S(1)}, u32[]{:S(2)}, u32[]{:S(2)}) collective-permute-start(bf16[4,256,512]{2,1,0:T(8,128)(2,1)S(1)} %get-tuple-element.49), channel_id=1, source_target_pairs={{0,1},{1,0},{2,3},{3,2},{4,5},{5,4},{6,7},{7,6},{8,9},{9,8},{10,11... | collective-permute-start | bytes 3145736 | tf_op jit(solution)/shard_map/ppermute | solution.py:54
  230.2 8.7 %gate_input_grad.1 = (bf16[4,512,256]{2,1,0:T(8,128)(2,1)S(1)}, bf16[4,512,256]{2,1,0:T(8,128)(2,1)S(1)}) custom-call(s32[4]{0:T(128)S(1)} %pad_add_fusion.meta, s32[288]{0:T(512)S(1)} %reduce.slots, bf16[18,128,128]{2,1,0:T(8,128)(2,1)S(1)} %copy-done.38, bf16[18,128,128]{2,1,0:T(8,128)(2,1)S(1)} %copy-done.16, bf16[18,128,128]{2,1,0:T(8,128)(2,1)S(1)} %copy-done.19, ...), custom_call_target="tpu_custom_call" | custom-call | flops 3758096384 | bytes 8388608 | tf_op jit(solution)/shard_map/gate_input_grad/pallas_call | solution.py:298
  239.0 15.3 %gate_tile_grad.1 = (bf16[18,128,128]{2,1,0:T(8,128)(2,1)S(1)}, bf16[18,128,128]{2,1,0:T(8,128)(2,1)S(1)}, bf16[9,128,128]{2,1,0:T(8,128)(2,1)S(1)}, bf16[9,128,...) custom-call(s32[4]{0:T(128)S(1)} %pad_add_fusion.meta, s32[288]{0:T(512)S(1)} %reduce.slots, ...), custom_call_target="tpu_custom_call" | custom-call | flops 3758096384 | bytes 9437184 | tf_op jit(solution)/shard_map/gate_tile_grad/pallas_call | solution.py:246
  254.6 1.4 collective-permute-start.58
  256.0 15.3 %up_tile_grad.1 = (bf16[18,128,128]{2,1,0:T(8,128)(2,1)S(1)}, bf16[18,128,128]{2,1,0:T(8,128)(2,1)S(1)}, bf16[9,128,128]{2,1,0:T(8,128)(2,1)S(1)}, bf16[9,128,12...) custom-call(s32[4]{0:T(128)S(1)} %pad_add_fusion.meta, s32[288]{0:T(512)S(1)} %reduce.1.slots, ...), custom_call_target="tpu_custom_call" | custom-call | flops 3758096384 | bytes 9437184 | tf_op jit(solution)/shard_map/up_tile_grad/pallas_call | solution.py:246
  271.5 1.5 collective-permute-start.62
  273.2 1.4 collective-permute-start.61
  274.7 4.2 %collective-permute-done.64 = bf16[9,128,128]{2,1,0:T(8,128)(2,1)S(1)} collective-permute-done((bf16[9,128,128]{2,1,0:T(8,128)(2,1)S(1)}, bf16[9,128,128]{2,1,0:T(8,128)(2,1)S(1)}, u32[]{:S(2)}, u32[]{:S(2)}) %collective-permute-start.64) | collective-permute-done | bytes 294944 | tf_op jit(solution)/shard_map/ppermute | solution.py:28
  282.1 3.3 %collective-permute-start.55 = (bf16[128,512]{1,0:T(8,128)(2,1)S(1)}, bf16[128,512]{1,0:T(8,128)(2,1)S(1)}, u32[]{:S(2)}, u32[]{:S(2)}) collective-permute-start(bf16[128,512]{1,0:T(8,128)(2,1)S(1)} %get-tuple-element.71), channel_id=1, source_target_pairs={{0,6},{2,0},{4,2},{6,4},{1,7},{3,1},{5,3},{7,5},{8,14},{10,8},{12,... | collective-permute-start | bytes 393224 | tf_op jit(solution)/shard_map/ppermute | solution.py:28
  285.7 2.2 collective-permute-done.53
  287.9 2.8 collective-permute-start.44
  290.8 2.4 collective-permute-done.42
  293.5 1.2 collective-permute-start.54
  294.8 1.5 collective-permute-start.45
  296.4 1.1 add_convert_fusion.3
  300.7 3.2 %collective-permute-done.45 = bf16[512,256]{1,0:T(8,128)(2,1)S(1)} collective-permute-done((bf16[512,256]{1,0:T(8,128)(2,1)S(1)}, bf16[512,256]{1,0:T(8,128)(2,1)S(1)}, u32[]{:S(2)}, u32[]{:S(2)}) %collective-permute-start.45) | collective-permute-done | bytes 262176 | tf_op jit(solution)/shard_map/ppermute | solution.py:28
  304.1 5.7 %collective-permute-start.46 = (bf16[256,256]{1,0:T(8,128)(2,1)S(1)}, bf16[256,256]{1,0:T(8,128)(2,1)S(1)}, u32[]{:S(2)}, u32[]{:S(2)}) collective-permute-start(bf16[256,256]{1,0:T(8,128)(2,1)S(1)} %get-tuple-element.76), channel_id=1, source_target_pairs={{9,0},{24,1},{0,8},{17,9},{8,16},{25,17},{1,24},{16,25},{11,2},{26... | collective-permute-start | bytes 393224 | tf_op jit(solution)/shard_map/ppermute | solution.py:371
  309.7 10.5 %collective-permute-start.47 = (bf16[256,256]{1,0:T(8,128)(2,1)S(1)}, bf16[256,256]{1,0:T(8,128)(2,1)S(1)}, u32[]{:S(2)}, u32[]{:S(2)}) collective-permute-start(bf16[256,256]{1,0:T(8,128)(2,1)S(1)} %get-tuple-element.77), channel_id=1, source_target_pairs={{0,0},{17,1},{8,8},{25,9},{1,16},{16,17},{9,24},{24,25},{2,2},{19,... | collective-permute-start | bytes 393224 | tf_op jit(solution)/shard_map/ppermute | solution.py:371
  320.2 1.1 add_convert_fusion.2
  (276 shorter events, 54.9 us)
Async XLA Ops:
  1.6 9.7 %collective-permute-start = (bf16[256,256]{1,0:T(8,128)(2,1)S(1)}, bf16[256,256]{1,0:T(8,128)(2,1)S(1)}, u32[]{:S(2)}, u32[]{:S(2)}) collective-permute-start(bf16[256,256]{1,0:T(8,128)(2,1)S(1)} %get-tuple-element.79), channel_id=1, source_target_pairs={{0,0},{1,17},{8,8},{9,25},{16,1},{17,16},{24,9},{25,24},{2,2},{3,1... | collective-permute-start | bytes 393224 | tf_op jit(solution)/shard_map/ppermute | solution.py:334
  8.0 5.7 %collective-permute-start.1 = (bf16[256,256]{1,0:T(8,128)(2,1)S(1)}, bf16[256,256]{1,0:T(8,128)(2,1)S(1)}, u32[]{:S(2)}, u32[]{:S(2)}) collective-permute-start(bf16[256,256]{1,0:T(8,128)(2,1)S(1)} %get-tuple-element.78), channel_id=1, source_target_pairs={{0,9},{1,24},{8,0},{9,17},{16,8},{17,25},{24,1},{25,16},{2,11},{3,... | collective-permute-start | bytes 393224 | tf_op jit(solution)/shard_map/ppermute | solution.py:335
  8.8 9.7 %collective-permute-start.19 = (bf16[256,512]{1,0:T(8,128)(2,1)}, bf16[256,512]{1,0:T(8,128)(2,1)S(1)}, u32[]{:S(2)}, u32[]{:S(2)}) collective-permute-start(bf16[256,512]{1,0:T(8,128)(2,1)} %param.6), channel_id=1, source_target_pairs={{0,0},{2,32},{4,64},{6,96},{32,2},{34,34},{36,66},{38,98},{64,4},{... | collective-permute-start | bytes 786440 | tf_op jit(solution)/shard_map/ppermute | solution.py:336
  13.7 19.9 %collective-permute-start.2 = (bf16[512,256]{1,0:T(8,128)(2,1)S(1)}, bf16[512,256]{1,0:T(8,128)(2,1)S(1)}, u32[]{:S(2)}, u32[]{:S(2)}) collective-permute-start(bf16[512,256]{1,0:T(8,128)(2,1)S(1)} %constant_dynamic-update-slice_fusion.refs_0_), channel_id=1, source_target_pairs={{0,2},{2,4},{4,6},{6,0},{1,3},{3,5},{5,7},{7,1},{8,10},{10,12},{12... | collective-permute-start | bytes 786440 | tf_op jit(solution)/shard_map/ppermute | solution.py:28
  15.0 18.6 %collective-permute-start.3 = (bf16[512,256]{1,0:T(8,128)(2,1)S(1)}, bf16[512,256]{1,0:T(8,128)(2,1)S(1)}, u32[]{:S(2)}, u32[]{:S(2)}) collective-permute-start(bf16[512,256]{1,0:T(8,128)(2,1)S(1)} %constant_dynamic-update-slice_fusion.refs_0_), channel_id=1, source_target_pairs={{0,6},{2,0},{4,2},{6,4},{1,7},{3,1},{5,3},{7,5},{8,14},{10,8},{12,... | collective-permute-start | bytes 786440 | tf_op jit(solution)/shard_map/ppermute | solution.py:28
  16.4 17.3 %collective-permute-start.6 = (bf16[512,256]{1,0:T(8,128)(2,1)S(1)}, bf16[512,256]{1,0:T(8,128)(2,1)S(1)}, u32[]{:S(2)}, u32[]{:S(2)}) collective-permute-start(bf16[512,256]{1,0:T(8,128)(2,1)S(1)} %constant_dynamic-update-slice_fusion.refs_0_), channel_id=1, source_target_pairs={{0,1},{1,0},{2,3},{3,2},{4,5},{5,4},{6,7},{7,6},{8,9},{9,8},{10,11... | collective-permute-start | bytes 786440 | tf_op jit(solution)/shard_map/ppermute | solution.py:54
  17.0 39.7 %collective-permute-start.11 = (bf16[18,128,128]{2,1,0:T(8,128)(2,1)}, bf16[18,128,128]{2,1,0:T(8,128)(2,1)S(1)}, u32[]{:S(2)}, u32[]{:S(2)}) collective-permute-start(bf16[18,128,128]{2,1,0:T(8,128)(2,1)} %refs_0_.2), channel_id=1, source_target_pairs={{0,32},{32,64},{64,96},{96,0},{1,33},{33,65},{65,97},{97,1},{2,34}... | collective-permute-start | bytes 1769480 | tf_op jit(solution)/shard_map/ppermute | solution.py:28
  18.5 38.2 %collective-permute-start.12 = (bf16[18,128,128]{2,1,0:T(8,128)(2,1)}, bf16[18,128,128]{2,1,0:T(8,128)(2,1)S(1)}, u32[]{:S(2)}, u32[]{:S(2)}) collective-permute-start(bf16[18,128,128]{2,1,0:T(8,128)(2,1)} %refs_0_.2), channel_id=1, source_target_pairs={{0,96},{32,0},{64,32},{96,64},{1,97},{33,1},{65,33},{97,65},{2,98}... | collective-permute-start | bytes 1769480 | tf_op jit(solution)/shard_map/ppermute | solution.py:28
  33.6 13.6 %collective-permute-start.20 = (bf16[256,512]{1,0:T(8,128)(2,1)S(1)}, bf16[256,512]{1,0:T(8,128)(2,1)S(1)}, u32[]{:S(2)}, u32[]{:S(2)}) collective-permute-start(bf16[256,512]{1,0:T(8,128)(2,1)S(1)} %collective-permute-done.19.refs_0_), channel_id=1, source_target_pairs={{0,2},{2,4},{4,6},{6,0},{1,3},{3,5},{5,7},{7,1},{8,10},{10,12},{12... | collective-permute-start | bytes 786440 | tf_op jit(solution)/shard_map/ppermute | solution.py:28
  33.6 10.8 %collective-permute-start.4 = (bf16[256,256]{1,0:T(8,128)(2,1)S(1)}, bf16[256,256]{1,0:T(8,128)(2,1)S(1)}, u32[]{:S(2)}, u32[]{:S(2)}) collective-permute-start(bf16[256,256]{1,0:T(8,128)(2,1)S(1)} %slice.216), channel_id=1, source_target_pairs={{0,2},{2,4},{4,6},{6,0},{1,3},{3,5},{5,7},{7,1},{8,10},{10,12},{12... | collective-permute-start | bytes 393224 | tf_op jit(solution)/shard_map/ppermute | solution.py:28
  34.4 10.0 %collective-permute-start.5 = (bf16[256,256]{1,0:T(8,128)(2,1)S(1)}, bf16[256,256]{1,0:T(8,128)(2,1)S(1)}, u32[]{:S(2)}, u32[]{:S(2)}) collective-permute-start(bf16[256,256]{1,0:T(8,128)(2,1)S(1)} %slice.217), channel_id=1, source_target_pairs={{0,6},{2,0},{4,2},{6,4},{1,7},{3,1},{5,3},{7,5},{8,14},{10,8},{12,... | collective-permute-start | bytes 393224 | tf_op jit(solution)/shard_map/ppermute | solution.py:28
  44.4 15.8 %collective-permute-start.29 = (bf16[18,128,128]{2,1,0:T(8,128)(2,1)}, bf16[18,128,128]{2,1,0:T(8,128)(2,1)S(1)}, u32[]{:S(2)}, u32[]{:S(2)}) collective-permute-start(bf16[18,128,128]{2,1,0:T(8,128)(2,1)} %refs_0_.3), channel_id=1, source_target_pairs={{0,8},{8,16},{16,24},{24,0},{1,9},{9,17},{17,25},{25,1},{2,10},{10... | collective-permute-start | bytes 1769480 | tf_op jit(solution)/shard_map/ppermute | solution.py:28
  44.4 18.5 %collective-permute-start.30 = (bf16[18,128,128]{2,1,0:T(8,128)(2,1)}, bf16[18,128,128]{2,1,0:T(8,128)(2,1)S(1)}, u32[]{:S(2)}, u32[]{:S(2)}) collective-permute-start(bf16[18,128,128]{2,1,0:T(8,128)(2,1)} %refs_0_.3), channel_id=1, source_target_pairs={{0,24},{8,0},{16,8},{24,16},{1,25},{9,1},{17,9},{25,17},{2,26},{10... | collective-permute-start | bytes 1769480 | tf_op jit(solution)/shard_map/ppermute | solution.py:28
  47.1 5.5 %collective-permute-start.21 = (bf16[256,512]{1,0:T(8,128)(2,1)S(1)}, bf16[256,512]{1,0:T(8,128)(2,1)}, u32[]{:S(2)}, u32[]{:S(2)}) collective-permute-start(bf16[256,512]{1,0:T(8,128)(2,1)S(1)} %collective-permute-done.19.refs_0_), channel_id=1, source_target_pairs={{0,6},{2,0},{4,2},{6,4},{1,7},{3,1},{5,3},{7,5},{8,14},{10,8},{12,... | collective-permute-start | bytes 786440 | tf_op jit(solution)/shard_map/ppermute | solution.py:28
  52.6 6.9 %collective-permute-start.24 = (bf16[256,512]{1,0:T(8,128)(2,1)S(1)}, bf16[256,512]{1,0:T(8,128)(2,1)S(1)}, u32[]{:S(2)}, u32[]{:S(2)}) collective-permute-start(bf16[256,512]{1,0:T(8,128)(2,1)S(1)} %collective-permute-done.19.refs_0_), channel_id=1, source_target_pairs={{0,1},{1,0},{2,3},{3,2},{4,5},{5,4},{6,7},{7,6},{8,9},{9,8},{10,11... | collective-permute-start | bytes 786440 | tf_op jit(solution)/shard_map/ppermute | solution.py:54
  56.7 7.6 %collective-permute-start.7 = (bf16[512,256]{1,0:T(8,128)(2,1)S(1)}, bf16[512,256]{1,0:T(8,128)(2,1)S(1)}, u32[]{:S(2)}, u32[]{:S(2)}) collective-permute-start(bf16[512,256]{1,0:T(8,128)(2,1)S(1)} %collective-permute-done.2.refs_1_), channel_id=1, source_target_pairs={{0,1},{1,0},{2,3},{3,2},{4,5},{5,4},{6,7},{7,6},{8,9},{9,8},{10,11... | collective-permute-start | bytes 786440 | tf_op jit(solution)/shard_map/ppermute | solution.py:54
  56.7 8.3 %collective-permute-start.8 = (bf16[512,256]{1,0:T(8,128)(2,1)S(1)}, bf16[512,256]{1,0:T(8,128)(2,1)S(1)}, u32[]{:S(2)}, u32[]{:S(2)}) collective-permute-start(bf16[512,256]{1,0:T(8,128)(2,1)S(1)} %collective-permute-done.3.refs_2_), channel_id=1, source_target_pairs={{0,1},{1,0},{2,3},{3,2},{4,5},{5,4},{6,7},{7,6},{8,9},{9,8},{10,11... | collective-permute-start | bytes 786440 | tf_op jit(solution)/shard_map/ppermute | solution.py:54
  60.2 19.7 %collective-permute-start.13 = (bf16[9,128,128]{2,1,0:T(8,128)(2,1)}, bf16[9,128,128]{2,1,0:T(8,128)(2,1)S(1)}, u32[]{:S(2)}, u32[]{:S(2)}) collective-permute-start(bf16[9,128,128]{2,1,0:T(8,128)(2,1)} %slice.218), channel_id=1, source_target_pairs={{0,32},{32,64},{64,96},{96,0},{1,33},{33,65},{65,97},{97,1},{2,34}... | collective-permute-start | bytes 884744 | tf_op jit(solution)/shard_map/ppermute | solution.py:28
  60.2 21.0 %collective-permute-start.14 = (bf16[9,128,128]{2,1,0:T(8,128)(2,1)}, bf16[9,128,128]{2,1,0:T(8,128)(2,1)S(1)}, u32[]{:S(2)}, u32[]{:S(2)}) collective-permute-start(bf16[9,128,128]{2,1,0:T(8,128)(2,1)} %slice.219), channel_id=1, source_target_pairs={{0,96},{32,0},{64,32},{96,64},{1,97},{33,1},{65,33},{97,65},{2,98}... | collective-permute-start | bytes 884744 | tf_op jit(solution)/shard_map/ppermute | solution.py:28
  62.9 5.5 %collective-permute-start.9 = (bf16[256,256]{1,0:T(8,128)(2,1)S(1)}, bf16[256,256]{1,0:T(8,128)(2,1)S(1)}, u32[]{:S(2)}, u32[]{:S(2)}) collective-permute-start(bf16[256,256]{1,0:T(8,128)(2,1)S(1)} %collective-permute-done.4.refs_3_), channel_id=1, source_target_pairs={{0,1},{1,0},{2,3},{3,2},{4,5},{5,4},{6,7},{7,6},{8,9},{9,8},{10,11... | collective-permute-start | bytes 393224 | tf_op jit(solution)/shard_map/ppermute | solution.py:54
  65.8 10.8 %collective-permute-start.25 = (bf16[256,512]{1,0:T(8,128)(2,1)S(1)}, bf16[256,512]{1,0:T(8,128)(2,1)S(1)}, u32[]{:S(2)}, u32[]{:S(2)}) collective-permute-start(bf16[256,512]{1,0:T(8,128)(2,1)S(1)} %collective-permute-done.20.refs_1_), channel_id=1, source_target_pairs={{0,1},{1,0},{2,3},{3,2},{4,5},{5,4},{6,7},{7,6},{8,9},{9,8},{10,11... | collective-permute-start | bytes 786440 | tf_op jit(solution)/shard_map/ppermute | solution.py:54
  69.1 6.6 %collective-permute-start.22 = (bf16[128,512]{1,0:T(8,128)(2,1)}, bf16[128,512]{1,0:T(8,128)(2,1)}, u32[]{:S(2)}, u32[]{:S(2)}) collective-permute-start(bf16[128,512]{1,0:T(8,128)(2,1)} %slice.220), channel_id=1, source_target_pairs={{0,2},{2,4},{4,6},{6,0},{1,3},{3,5},{5,7},{7,1},{8,10},{10,12},{12... | collective-permute-start | bytes 393224 | tf_op jit(solution)/shard_map/ppermute | solution.py:28
  69.8 6.8 %collective-permute-start.23 = (bf16[128,512]{1,0:T(8,128)(2,1)}, bf16[128,512]{1,0:T(8,128)(2,1)}, u32[]{:S(2)}, u32[]{:S(2)}) collective-permute-start(bf16[128,512]{1,0:T(8,128)(2,1)} %slice.221), channel_id=1, source_target_pairs={{0,6},{2,0},{4,2},{6,4},{1,7},{3,1},{5,3},{7,5},{8,14},{10,8},{12,... | collective-permute-start | bytes 393224 | tf_op jit(solution)/shard_map/ppermute | solution.py:28
  75.7 31.5 %collective-permute-start.26 = (bf16[256,512]{1,0:T(8,128)(2,1)}, bf16[256,512]{1,0:T(8,128)(2,1)S(1)}, u32[]{:S(2)}, u32[]{:S(2)}) collective-permute-start(bf16[256,512]{1,0:T(8,128)(2,1)} %collective-permute-done.21.refs_2_), channel_id=1, source_target_pairs={{0,1},{1,0},{2,3},{3,2},{4,5},{5,4},{6,7},{7,6},{8,9},{9,8},{10,11... | collective-permute-start | bytes 786440 | tf_op jit(solution)/shard_map/ppermute | solution.py:54
  76.5 36.6 %collective-permute-start.31 = (bf16[9,128,128]{2,1,0:T(8,128)(2,1)}, bf16[9,128,128]{2,1,0:T(8,128)(2,1)}, u32[]{:S(2)}, u32[]{:S(2)}) collective-permute-start(bf16[9,128,128]{2,1,0:T(8,128)(2,1)} %slice.222), channel_id=1, source_target_pairs={{0,8},{8,16},{16,24},{24,0},{1,9},{9,17},{17,25},{25,1},{2,10},{10... | collective-permute-start | bytes 884744 | tf_op jit(solution)/shard_map/ppermute | solution.py:28
  77.3 35.9 %collective-permute-start.32 = (bf16[9,128,128]{2,1,0:T(8,128)(2,1)}, bf16[9,128,128]{2,1,0:T(8,128)(2,1)}, u32[]{:S(2)}, u32[]{:S(2)}) collective-permute-start(bf16[9,128,128]{2,1,0:T(8,128)(2,1)} %slice.223), channel_id=1, source_target_pairs={{0,24},{8,0},{16,8},{24,16},{1,25},{9,1},{17,9},{25,17},{2,26},{10... | collective-permute-start | bytes 884744 | tf_op jit(solution)/shard_map/ppermute | solution.py:28
  80.6 29.5 %collective-permute-start.27 = (bf16[128,512]{1,0:T(8,128)(2,1)}, bf16[128,512]{1,0:T(8,128)(2,1)}, u32[]{:S(2)}, u32[]{:S(2)}) collective-permute-start(bf16[128,512]{1,0:T(8,128)(2,1)} %collective-permute-done.22.refs_3_), channel_id=1, source_target_pairs={{0,1},{1,0},{2,3},{3,2},{4,5},{5,4},{6,7},{7,6},{8,9},{9,8},{10,11... | collective-permute-start | bytes 393224 | tf_op jit(solution)/shard_map/ppermute | solution.py:54
  81.9 31.2 %collective-permute-start.28 = (bf16[128,512]{1,0:T(8,128)(2,1)}, bf16[128,512]{1,0:T(8,128)(2,1)}, u32[]{:S(2)}, u32[]{:S(2)}) collective-permute-start(bf16[128,512]{1,0:T(8,128)(2,1)} %collective-permute-done.23.refs_4_), channel_id=1, source_target_pairs={{0,1},{1,0},{2,3},{3,2},{4,5},{5,4},{6,7},{7,6},{8,9},{9,8},{10,11... | collective-permute-start | bytes 393224 | tf_op jit(solution)/shard_map/ppermute | solution.py:54
  107.8 21.6 %collective-permute-start.15 = (bf16[128,1792]{1,0:T(8,128)(2,1)}, bf16[128,1792]{1,0:T(8,128)(2,1)}, u32[]{:S(2)}, u32[]{:S(2)}) collective-permute-start(bf16[128,1792]{1,0:T(8,128)(2,1)} %get-tuple-element.35), channel_id=1, source_target_pairs={{0,8},{8,16},{16,24},{24,0},{1,9},{9,17},{17,25},{25,1},{2,10},{10... | collective-permute-start | bytes 1376264 | tf_op jit(solution)/shard_map/ppermute | solution.py:28
  110.1 20.7 %collective-permute-start.17 = (bf16[128,1792]{1,0:T(8,128)(2,1)}, bf16[128,1792]{1,0:T(8,128)(2,1)S(1)}, u32[]{:S(2)}, u32[]{:S(2)}) collective-permute-start(bf16[128,1792]{1,0:T(8,128)(2,1)} %copy-done.39), channel_id=1, source_target_pairs={{0,24},{8,0},{16,8},{24,16},{1,25},{9,1},{17,9},{25,17},{2,26},{10... | collective-permute-start | bytes 1376264 | tf_op jit(solution)/shard_map/ppermute | solution.py:28
  126.7 12.2 %collective-permute-start.33 = (bf16[128,1792]{1,0:T(8,128)(2,1)S(1)}, bf16[128,1792]{1,0:T(8,128)(2,1)S(1)}, u32[]{:S(2)}, u32[]{:S(2)}) collective-permute-start(bf16[128,1792]{1,0:T(8,128)(2,1)S(1)} %get-tuple-element.40), channel_id=1, source_target_pairs={{0,32},{32,64},{64,96},{96,0},{1,33},{33,65},{65,97},{97,1},{2,34}... | collective-permute-start | bytes 1376264 | tf_op jit(solution)/shard_map/ppermute | solution.py:28
  126.8 12.4 %collective-permute-start.35 = (bf16[128,1792]{1,0:T(8,128)(2,1)S(1)}, bf16[128,1792]{1,0:T(8,128)(2,1)S(1)}, u32[]{:S(2)}, u32[]{:S(2)}) collective-permute-start(bf16[128,1792]{1,0:T(8,128)(2,1)S(1)} %get-tuple-element.42), channel_id=1, source_target_pairs={{0,96},{32,0},{64,32},{96,64},{1,97},{33,1},{65,33},{97,65},{2,98}... | collective-permute-start | bytes 1376264 | tf_op jit(solution)/shard_map/ppermute | solution.py:28
  130.8 21.4 %collective-permute-start.16 = (bf16[256,1792]{1,0:T(8,128)(2,1)S(1)}, bf16[256,1792]{1,0:T(8,128)(2,1)S(1)}, u32[]{:S(2)}, u32[]{:S(2)}) collective-permute-start(bf16[256,1792]{1,0:T(8,128)(2,1)S(1)} %pad_maximum_fusion), channel_id=1, source_target_pairs={{0,8},{8,16},{16,24},{24,0},{1,9},{9,17},{17,25},{25,1},{2,10},{10... | collective-permute-start | bytes 2752520 | tf_op jit(solution)/shard_map/ppermute | solution.py:28
  131.1 21.1 %collective-permute-start.18 = (bf16[256,1792]{1,0:T(8,128)(2,1)S(1)}, bf16[256,1792]{1,0:T(8,128)(2,1)S(1)}, u32[]{:S(2)}, u32[]{:S(2)}) collective-permute-start(bf16[256,1792]{1,0:T(8,128)(2,1)S(1)} %pad_maximum_fusion.1), channel_id=1, source_target_pairs={{0,24},{8,0},{16,8},{24,16},{1,25},{9,1},{17,9},{25,17},{2,26},{10... | collective-permute-start | bytes 2752520 | tf_op jit(solution)/shard_map/ppermute | solution.py:28
  139.0 21.1 %collective-permute-start.34 = (bf16[256,1792]{1,0:T(8,128)(2,1)S(1)}, bf16[256,1792]{1,0:T(8,128)(2,1)S(1)}, u32[]{:S(2)}, u32[]{:S(2)}) collective-permute-start(bf16[256,1792]{1,0:T(8,128)(2,1)S(1)} %pad_maximum_fusion.2), channel_id=1, source_target_pairs={{0,32},{32,64},{64,96},{96,0},{1,33},{33,65},{65,97},{97,1},{2,34}... | collective-permute-start | bytes 2752520 | tf_op jit(solution)/shard_map/ppermute | solution.py:28
  139.3 20.8 %collective-permute-start.36 = (bf16[256,1792]{1,0:T(8,128)(2,1)S(1)}, bf16[256,1792]{1,0:T(8,128)(2,1)S(1)}, u32[]{:S(2)}, u32[]{:S(2)}) collective-permute-start(bf16[256,1792]{1,0:T(8,128)(2,1)S(1)} %pad_maximum_fusion.3), channel_id=1, source_target_pairs={{0,96},{32,0},{64,32},{96,64},{1,97},{33,1},{65,33},{97,65},{2,98}... | collective-permute-start | bytes 2752520 | tf_op jit(solution)/shard_map/ppermute | solution.py:28
  163.6 20.1 %collective-permute-start.48 = (bf16[256,1792]{1,0:T(8,128)(2,1)S(1)}, bf16[256,1792]{1,0:T(8,128)(2,1)S(1)}, u32[]{:S(2)}, u32[]{:S(2)}) collective-permute-start(bf16[256,1792]{1,0:T(8,128)(2,1)S(1)} %get-tuple-element.47.refs_5_.own), channel_id=1, source_target_pairs={{0,32},{32,64},{64,96},{96,0},{1,33},{33,65},{65,97},{97,1},{2,34}... | collective-permute-start | bytes 2752520 | tf_op jit(solution)/shard_map/ppermute | solution.py:28
  163.6 20.9 %collective-permute-start.49 = (bf16[256,1792]{1,0:T(8,128)(2,1)S(1)}, bf16[256,1792]{1,0:T(8,128)(2,1)S(1)}, u32[]{:S(2)}, u32[]{:S(2)}) collective-permute-start(bf16[256,1792]{1,0:T(8,128)(2,1)S(1)} %get-tuple-element.47.refs_5_.own), channel_id=1, source_target_pairs={{0,96},{32,0},{64,32},{96,64},{1,97},{33,1},{65,33},{97,65},{2,98}... | collective-permute-start | bytes 2752520 | tf_op jit(solution)/shard_map/ppermute | solution.py:28
  166.3 22.6 %collective-permute-start.37 = (bf16[256,1792]{1,0:T(8,128)(2,1)S(1)}, bf16[256,1792]{1,0:T(8,128)(2,1)S(1)}, u32[]{:S(2)}, u32[]{:S(2)}) collective-permute-start(bf16[256,1792]{1,0:T(8,128)(2,1)S(1)} %get-tuple-element.44.refs_5_.own), channel_id=1, source_target_pairs={{0,8},{8,16},{16,24},{24,0},{1,9},{9,17},{17,25},{25,1},{2,10},{10... | collective-permute-start | bytes 2752520 | tf_op jit(solution)/shard_map/ppermute | solution.py:28
  166.3 24.4 %collective-permute-start.38 = (bf16[256,1792]{1,0:T(8,128)(2,1)S(1)}, bf16[256,1792]{1,0:T(8,128)(2,1)S(1)}, u32[]{:S(2)}, u32[]{:S(2)}) collective-permute-start(bf16[256,1792]{1,0:T(8,128)(2,1)S(1)} %get-tuple-element.44.refs_5_.own), channel_id=1, source_target_pairs={{0,24},{8,0},{16,8},{24,16},{1,25},{9,1},{17,9},{25,17},{2,26},{10... | collective-permute-start | bytes 2752520 | tf_op jit(solution)/shard_map/ppermute | solution.py:28
  184.5 16.1 %collective-permute-start.50 = (bf16[128,1792]{1,0:T(8,128)(2,1)}, bf16[128,1792]{1,0:T(8,128)(2,1)}, u32[]{:S(2)}, u32[]{:S(2)}) collective-permute-start(bf16[128,1792]{1,0:T(8,128)(2,1)} %slice.235), channel_id=1, source_target_pairs={{0,32},{32,64},{64,96},{96,0},{1,33},{33,65},{65,97},{97,1},{2,34}... | collective-permute-start | bytes 1376264 | tf_op jit(solution)/shard_map/ppermute | solution.py:28
  186.2 14.3 %collective-permute-start.51 = (bf16[128,1792]{1,0:T(8,128)(2,1)}, bf16[128,1792]{1,0:T(8,128)(2,1)}, u32[]{:S(2)}, u32[]{:S(2)}) collective-permute-start(bf16[128,1792]{1,0:T(8,128)(2,1)} %slice.236), channel_id=1, source_target_pairs={{0,96},{32,0},{64,32},{96,64},{1,97},{33,1},{65,33},{97,65},{2,98}... | collective-permute-start | bytes 1376264 | tf_op jit(solution)/shard_map/ppermute | solution.py:28
  190.6 39.5 %collective-permute-start.39 = (bf16[128,1792]{1,0:T(8,128)(2,1)}, bf16[128,1792]{1,0:T(8,128)(2,1)}, u32[]{:S(2)}, u32[]{:S(2)}) collective-permute-start(bf16[128,1792]{1,0:T(8,128)(2,1)} %slice.224), channel_id=1, source_target_pairs={{0,8},{8,16},{16,24},{24,0},{1,9},{9,17},{17,25},{25,1},{2,10},{10... | collective-permute-start | bytes 1376264 | tf_op jit(solution)/shard_map/ppermute | solution.py:28
  192.4 37.7 %collective-permute-start.40 = (bf16[128,1792]{1,0:T(8,128)(2,1)}, bf16[128,1792]{1,0:T(8,128)(2,1)}, u32[]{:S(2)}, u32[]{:S(2)}) collective-permute-start(bf16[128,1792]{1,0:T(8,128)(2,1)} %slice.225), channel_id=1, source_target_pairs={{0,24},{8,0},{16,8},{24,16},{1,25},{9,1},{17,9},{25,17},{2,26},{10... | collective-permute-start | bytes 1376264 | tf_op jit(solution)/shard_map/ppermute | solution.py:28
  215.2 66.0 %collective-permute-start.52 = (bf16[4,256,512]{2,1,0:T(8,128)(2,1)S(1)}, bf16[4,256,512]{2,1,0:T(8,128)(2,1)S(1)}, u32[]{:S(2)}, u32[]{:S(2)}) collective-permute-start(bf16[4,256,512]{2,1,0:T(8,128)(2,1)S(1)} %get-tuple-element.49), channel_id=1, source_target_pairs={{0,1},{1,0},{2,3},{3,2},{4,5},{5,4},{6,7},{7,6},{8,9},{9,8},{10,11... | collective-permute-start | bytes 3145736 | tf_op jit(solution)/shard_map/ppermute | solution.py:54
  238.9 43.2 %collective-permute-start.41 = (bf16[4,512,256]{2,1,0:T(8,128)(2,1)S(1)}, bf16[4,512,256]{2,1,0:T(8,128)(2,1)S(1)}, u32[]{:S(2)}, u32[]{:S(2)}) collective-permute-start(bf16[4,512,256]{2,1,0:T(8,128)(2,1)S(1)} %get-tuple-element.46), channel_id=1, source_target_pairs={{0,1},{1,0},{2,3},{3,2},{4,5},{5,4},{6,7},{7,6},{8,9},{9,8},{10,11... | collective-permute-start | bytes 3145736 | tf_op jit(solution)/shard_map/ppermute | solution.py:54
  254.4 17.1 %collective-permute-start.60 = (bf16[9,128,128]{2,1,0:T(8,128)(2,1)S(1)}, bf16[9,128,128]{2,1,0:T(8,128)(2,1)S(1)}, u32[]{:S(2)}, u32[]{:S(2)}) collective-permute-start(bf16[9,128,128]{2,1,0:T(8,128)(2,1)S(1)} %get-tuple-element.55), channel_id=1, source_target_pairs={{0,96},{32,0},{64,32},{96,64},{1,97},{33,1},{65,33},{97,65},{2,98}... | collective-permute-start | bytes 884744 | tf_op jit(solution)/shard_map/ppermute | solution.py:28
  254.6 18.6 %collective-permute-start.58 = (bf16[9,128,128]{2,1,0:T(8,128)(2,1)S(1)}, bf16[9,128,128]{2,1,0:T(8,128)(2,1)S(1)}, u32[]{:S(2)}, u32[]{:S(2)}) collective-permute-start(bf16[9,128,128]{2,1,0:T(8,128)(2,1)S(1)} %get-tuple-element.53), channel_id=1, source_target_pairs={{0,32},{32,64},{64,96},{96,0},{1,33},{33,65},{65,97},{97,1},{2,34}... | collective-permute-start | bytes 884744 | tf_op jit(solution)/shard_map/ppermute | solution.py:28
  271.4 7.5 %collective-permute-start.64 = (bf16[9,128,128]{2,1,0:T(8,128)(2,1)S(1)}, bf16[9,128,128]{2,1,0:T(8,128)(2,1)S(1)}, u32[]{:S(2)}, u32[]{:S(2)}) collective-permute-start(bf16[9,128,128]{2,1,0:T(8,128)(2,1)S(1)} %get-tuple-element.61), channel_id=1, source_target_pairs={{0,24},{8,0},{16,8},{24,16},{1,25},{9,1},{17,9},{25,17},{2,26},{10... | collective-permute-start | bytes 884744 | tf_op jit(solution)/shard_map/ppermute | solution.py:28
  271.5 8.7 %collective-permute-start.62 = (bf16[9,128,128]{2,1,0:T(8,128)(2,1)S(1)}, bf16[9,128,128]{2,1,0:T(8,128)(2,1)S(1)}, u32[]{:S(2)}, u32[]{:S(2)}) collective-permute-start(bf16[9,128,128]{2,1,0:T(8,128)(2,1)S(1)} %get-tuple-element.59), channel_id=1, source_target_pairs={{0,8},{8,16},{16,24},{24,0},{1,9},{9,17},{17,25},{25,1},{2,10},{10... | collective-permute-start | bytes 884744 | tf_op jit(solution)/shard_map/ppermute | solution.py:28
  273.2 21.6 %collective-permute-start.61 = (bf16[18,128,128]{2,1,0:T(8,128)(2,1)S(1)}, bf16[18,128,128]{2,1,0:T(8,128)(2,1)S(1)}, u32[]{:S(2)}, u32[]{:S(2)}) collective-permute-start(bf16[18,128,128]{2,1,0:T(8,128)(2,1)S(1)} %pad_maximum_fusion.5), channel_id=1, source_target_pairs={{0,96},{32,0},{64,32},{96,64},{1,97},{33,1},{65,33},{97,65},{2,98}... | collective-permute-start | bytes 1769480 | tf_op jit(solution)/shard_map/ppermute | solution.py:28
  278.9 17.5 %collective-permute-start.59 = (bf16[18,128,128]{2,1,0:T(8,128)(2,1)S(1)}, bf16[18,128,128]{2,1,0:T(8,128)(2,1)S(1)}, u32[]{:S(2)}, u32[]{:S(2)}) collective-permute-start(bf16[18,128,128]{2,1,0:T(8,128)(2,1)S(1)} %pad_maximum_fusion.4), channel_id=1, source_target_pairs={{0,32},{32,64},{64,96},{96,0},{1,33},{33,65},{65,97},{97,1},{2,34}... | collective-permute-start | bytes 1769480 | tf_op jit(solution)/shard_map/ppermute | solution.py:28
  280.3 40.0 %collective-permute-start.65 = (bf16[18,128,128]{2,1,0:T(8,128)(2,1)S(1)}, bf16[18,128,128]{2,1,0:T(8,128)(2,1)S(1)}, u32[]{:S(2)}, u32[]{:S(2)}) collective-permute-start(bf16[18,128,128]{2,1,0:T(8,128)(2,1)S(1)} %pad_maximum_fusion.7), channel_id=1, source_target_pairs={{0,24},{8,0},{16,8},{24,16},{1,25},{9,1},{17,9},{25,17},{2,26},{10... | collective-permute-start | bytes 1769480 | tf_op jit(solution)/shard_map/ppermute | solution.py:28
  281.5 6.4 %collective-permute-start.53 = (bf16[128,512]{1,0:T(8,128)(2,1)S(1)}, bf16[128,512]{1,0:T(8,128)(2,1)S(1)}, u32[]{:S(2)}, u32[]{:S(2)}) collective-permute-start(bf16[128,512]{1,0:T(8,128)(2,1)S(1)} %get-tuple-element.70), channel_id=1, source_target_pairs={{0,2},{2,4},{4,6},{6,0},{1,3},{3,5},{5,7},{7,1},{8,10},{10,12},{12... | collective-permute-start | bytes 393224 | tf_op jit(solution)/shard_map/ppermute | solution.py:28
  282.1 5.8 %collective-permute-start.55 = (bf16[128,512]{1,0:T(8,128)(2,1)S(1)}, bf16[128,512]{1,0:T(8,128)(2,1)S(1)}, u32[]{:S(2)}, u32[]{:S(2)}) collective-permute-start(bf16[128,512]{1,0:T(8,128)(2,1)S(1)} %get-tuple-element.71), channel_id=1, source_target_pairs={{0,6},{2,0},{4,2},{6,4},{1,7},{3,1},{5,3},{7,5},{8,14},{10,8},{12,... | collective-permute-start | bytes 393224 | tf_op jit(solution)/shard_map/ppermute | solution.py:28
  287.9 5.3 %collective-permute-start.42 = (bf16[256,256]{1,0:T(8,128)(2,1)S(1)}, bf16[256,256]{1,0:T(8,128)(2,1)S(1)}, u32[]{:S(2)}, u32[]{:S(2)}) collective-permute-start(bf16[256,256]{1,0:T(8,128)(2,1)S(1)} %get-tuple-element.64), channel_id=1, source_target_pairs={{0,2},{2,4},{4,6},{6,0},{1,3},{3,5},{5,7},{7,1},{8,10},{10,12},{12... | collective-permute-start | bytes 393224 | tf_op jit(solution)/shard_map/ppermute | solution.py:28
  287.9 5.6 %collective-permute-start.44 = (bf16[256,256]{1,0:T(8,128)(2,1)S(1)}, bf16[256,256]{1,0:T(8,128)(2,1)S(1)}, u32[]{:S(2)}, u32[]{:S(2)}) collective-permute-start(bf16[256,256]{1,0:T(8,128)(2,1)S(1)} %get-tuple-element.65), channel_id=1, source_target_pairs={{0,6},{2,0},{4,2},{6,4},{1,7},{3,1},{5,3},{7,5},{8,14},{10,8},{12,... | collective-permute-start | bytes 393224 | tf_op jit(solution)/shard_map/ppermute | solution.py:28
  293.5 6.4 %collective-permute-start.54 = (bf16[256,512]{1,0:T(8,128)(2,1)S(1)}, bf16[256,512]{1,0:T(8,128)(2,1)S(1)}, u32[]{:S(2)}, u32[]{:S(2)}) collective-permute-start(bf16[256,512]{1,0:T(8,128)(2,1)S(1)} %pad_maximum_fusion.10), channel_id=1, source_target_pairs={{0,2},{2,4},{4,6},{6,0},{1,3},{3,5},{5,7},{7,1},{8,10},{10,12},{12... | collective-permute-start | bytes 786440 | tf_op jit(solution)/shard_map/ppermute | solution.py:28
  294.8 9.1 %collective-permute-start.45 = (bf16[512,256]{1,0:T(8,128)(2,1)S(1)}, bf16[512,256]{1,0:T(8,128)(2,1)S(1)}, u32[]{:S(2)}, u32[]{:S(2)}) collective-permute-start(bf16[512,256]{1,0:T(8,128)(2,1)S(1)} %pad_maximum_fusion.9), channel_id=1, source_target_pairs={{0,6},{2,0},{4,2},{6,4},{1,7},{3,1},{5,3},{7,5},{8,14},{10,8},{12,... | collective-permute-start | bytes 786440 | tf_op jit(solution)/shard_map/ppermute | solution.py:28
  296.4 7.6 %collective-permute-start.43 = (bf16[512,256]{1,0:T(8,128)(2,1)S(1)}, bf16[512,256]{1,0:T(8,128)(2,1)S(1)}, u32[]{:S(2)}, u32[]{:S(2)}) collective-permute-start(bf16[512,256]{1,0:T(8,128)(2,1)S(1)} %pad_maximum_fusion.8), channel_id=1, source_target_pairs={{0,2},{2,4},{4,6},{6,0},{1,3},{3,5},{5,7},{7,1},{8,10},{10,12},{12... | collective-permute-start | bytes 786440 | tf_op jit(solution)/shard_map/ppermute | solution.py:28
  298.5 21.8 %collective-permute-start.63 = (bf16[18,128,128]{2,1,0:T(8,128)(2,1)S(1)}, bf16[18,128,128]{2,1,0:T(8,128)(2,1)S(1)}, u32[]{:S(2)}, u32[]{:S(2)}) collective-permute-start(bf16[18,128,128]{2,1,0:T(8,128)(2,1)S(1)} %pad_maximum_fusion.6), channel_id=1, source_target_pairs={{0,8},{8,16},{16,24},{24,0},{1,9},{9,17},{17,25},{25,1},{2,10},{10... | collective-permute-start | bytes 1769480 | tf_op jit(solution)/shard_map/ppermute | solution.py:28
  300.0 22.1 %collective-permute-start.57 = (bf16[256,512]{1,0:T(8,128)(2,1)S(1)}, bf16[256,512]{1,0:T(8,128)(2,1)S(1)}, u32[]{:S(2)}, u32[]{:S(2)}) collective-permute-start(bf16[256,512]{1,0:T(8,128)(2,1)S(1)} %fusion.1), channel_id=1, source_target_pairs={{0,0},{2,32},{4,64},{6,96},{32,2},{34,34},{36,66},{38,98},{64,4},{... | collective-permute-start | bytes 786440 | tf_op jit(solution)/shard_map/ppermute | solution.py:375
  304.1 17.3 %collective-permute-start.46 = (bf16[256,256]{1,0:T(8,128)(2,1)S(1)}, bf16[256,256]{1,0:T(8,128)(2,1)S(1)}, u32[]{:S(2)}, u32[]{:S(2)}) collective-permute-start(bf16[256,256]{1,0:T(8,128)(2,1)S(1)} %get-tuple-element.76), channel_id=1, source_target_pairs={{9,0},{24,1},{0,8},{17,9},{8,16},{25,17},{1,24},{16,25},{11,2},{26... | collective-permute-start | bytes 393224 | tf_op jit(solution)/shard_map/ppermute | solution.py:371
  309.7 12.4 %collective-permute-start.47 = (bf16[256,256]{1,0:T(8,128)(2,1)S(1)}, bf16[256,256]{1,0:T(8,128)(2,1)S(1)}, u32[]{:S(2)}, u32[]{:S(2)}) collective-permute-start(bf16[256,256]{1,0:T(8,128)(2,1)S(1)} %get-tuple-element.77), channel_id=1, source_target_pairs={{0,0},{17,1},{8,8},{25,9},{1,16},{16,17},{9,24},{24,25},{2,2},{19,... | collective-permute-start | bytes 393224 | tf_op jit(solution)/shard_map/ppermute | solution.py:371
  (72 other events, 677.7 us)
